TPU v7x, 32 devices: a whole 2x2x4 slice. The times are simulated.
32 devices in a mesh: dp: 4 (over z), ep: 2 (over core), tp: 4 (over y, x).
Axes of the slice: x: 2, y: 2, z: 4, core: 2. Of those that a mesh axis runs over, the one named last changes fastest.
Arguments:
- activations: bfloat16 [4096, 1536], P(('dp', 'ep', 'tp')), may hold values from -6 to 6
- segments: int32 [8, 512], P(('dp', 'ep')), may hold values from 0 to 3, never falling along the last dimension, each value on 1 to 256 neighbouring positions
- routes: int32 [4096, 8], P(('dp', 'ep', 'tp')), may hold values from 0 to 19, all different within a row; in each aligned block of 128 rows (0 to 127, 128 to 255, ...) at most 52 rows name the same one
- attn_gain: float32 [1536], replicated, may hold values from 0.25 to 1.75
- w_query: bfloat16 [1536, 1536], P(None, 'tp'), may hold values from -0.15625 to 0.15625
- key_value_weight: bfloat16 [1536, 8, 128], P(None, 'tp'), may hold values from -0.15625 to 0.15625
- w_output: bfloat16 [1536, 1536], P('tp'), may hold values from -0.625 to 0.625
- moe_gain: float32 [1536], replicated, may hold values from 0.25 to 1.75
- w_router: bfloat16 [1536, 20], replicated, may hold values from -0.079589844 to 0.079589844
- w_in: bfloat16 [20, 2, 512, 1536], P('ep', None, 'tp'), may hold values from -0.15625 to 0.15625
- w_out: bfloat16 [20, 512, 1536], P('ep', 'tp'), may hold values from -1 to 1
- out_cotangent: bfloat16 [4096, 1536], P(('dp', 'ep', 'tp')), may hold values from -8 to 8
Outputs:
- block_out: bfloat16 [4096, 1536], P(('dp', 'ep', 'tp'))
- grad_input: float32 [4096, 1536], P(('dp', 'ep', 'tp'))
- grad_attn_gain: float32 [1536], replicated
- grad_w_query: float32 [1536, 1536], P(('dp', 'ep'), 'tp')
- grad_w_keyval: float32 [1536, 8, 128], P(('dp', 'ep'), 'tp')
- grad_w_output: float32 [1536, 1536], P('tp', ('dp', 'ep'))
- grad_moe_gain: float32 [1536], replicated
- grad_w_router: float32 [1536, 20], replicated
- grad_w_in: float32 [20, 2, 512, 1536], P('ep', None, 'tp', 'dp')
- grad_w_out: float32 [20, 512, 1536], P('ep', 'tp', 'dp')
Inputs may be any that keep to these rules, and one draw needn't show every extreme that they name: `segments`: along each sequence the numbers never fall; no document is longer than 256 positions and some document reaches that length. A token's 8 experts differ. Within the routes of one device's tokens (aligned blocks of 128 rows) no expert is named more than 52 times, a bound that some block reaches.
All inputs are finite; a program needn't handle non-finite values.
Results may differ from a plain program's by a relative error of at most 0.023.
Values may be sent and summed in bfloat16 or wider, within the bound.
A program may use at most 256 MiB of HBM per device.

v0:
```python
import math

import jax
import jax.numpy as jnp
from jax import lax
from jax.sharding import PartitionSpec as P

eps_norm = 1e-05
rope_base = 10000.0
neg_fill = -1000000000.0


def cut_along(value, dim, devices):
    shape = value.shape
    blocks = value.reshape(*shape[:dim], devices, shape[dim] // devices, *shape[dim + 1 :])
    return jnp.moveaxis(blocks, dim, 0)


def summed_on_arrival(value, axis, dim):
    blocks = cut_along(value, dim, lax.axis_size(axis))
    arrived = lax.all_to_all(blocks, axis, split_axis=0, concat_axis=0, tiled=True)
    return arrived.astype(jnp.float32).sum(axis=0)


def sent_together(arrays, axis, dim, along):
    widths = [math.prod(a.shape[along:]) for a in arrays]
    both = jnp.concatenate(
        [a.reshape(*a.shape[:along], w) for a, w in zip(arrays, widths)], axis=along
    )
    whole = summed_on_arrival(both, axis, dim)
    blocks = jnp.split(whole, [sum(widths[:k]) for k in range(1, len(widths))], axis=along)
    return tuple(
        (b.reshape(*whole.shape[:along], *a.shape[along:]) for a, b in zip(arrays, blocks))
    )


def rope_tables(length, head_size):
    half_size = head_size // 2
    frequency = jnp.exp(
        jnp.arange(half_size, dtype=jnp.float32) * (-2.0 * math.log(rope_base) / head_size)
    )
    angles = jnp.arange(length, dtype=jnp.float32)[:, None] * frequency[None, :]
    return (jnp.cos(angles)[:, None, :], jnp.sin(angles)[:, None, :])


def apply_rotation(tensor, cosine_rows, sine_rows):
    half_size = tensor.shape[-1] // 2
    first = tensor[..., :half_size]
    second = tensor[..., half_size:]
    return jnp.concatenate(
        [first * cosine_rows - second * sine_rows, second * cosine_rows + first * sine_rows],
        axis=-1,
    )


def normalize(matrix):
    factor = lax.rsqrt(jnp.mean(matrix * matrix, axis=-1, keepdims=True) + eps_norm)
    return (matrix * factor, factor)


def norm_back(grad_normed, normed_hat, factor, gain):
    grad_hat = grad_normed * gain
    grad_inner = jnp.mean(grad_hat * normed_hat, axis=-1, keepdims=True)
    return (
        factor * (grad_hat - normed_hat * grad_inner),
        jnp.sum(grad_normed * normed_hat, axis=0),
    )


def deliver(blocks):
    arrived = lax.all_to_all(blocks, "ep", split_axis=0, concat_axis=0, tiled=True)
    return lax.all_gather(arrived, "tp", axis=0, tiled=True)


def collect(make_term, source_count):
    tp_count = lax.axis_size("tp")
    ep_count = source_count // tp_count
    summed = lax.psum_scatter(
        make_term(jnp.int32(0), ep_count * lax.axis_size("tp")).astype(jnp.bfloat16),
        "tp",
        scatter_dimension=0,
        tiled=True,
    ).astype(jnp.float32)
    return lax.all_to_all(
        summed.astype(jnp.bfloat16), "ep", split_axis=0, concat_axis=0, tiled=True
    ).astype(summed.dtype)


def per_device(
    activations,
    segments,
    routes,
    attn_gain,
    w_query,
    key_value_weight,
    w_output,
    moe_gain,
    w_router,
    w_in,
    w_out,
    out_cotangent,
):
    row_count, width = activations.shape
    tp_count = lax.axis_size("tp")
    seq_len = row_count * tp_count
    head_size = key_value_weight.shape[2] // 2
    kv_heads = key_value_weight.shape[1]
    q_heads = w_query.shape[1] // head_size
    heads_per_group = q_heads // kv_heads
    top_count = routes.shape[1]
    expert_count = w_router.shape[1]
    local_experts = w_in.shape[0]
    capacity = (row_count * top_count + expert_count - 1) // expert_count
    score_scale = 1.0 / math.sqrt(head_size)
    cosine_rows, sine_rows = rope_tables(seq_len, head_size)
    x_float = activations.astype(jnp.float32)
    hat_one, factor_one = normalize(x_float)
    normed_one = (hat_one * attn_gain).astype(jnp.bfloat16)
    full_rows = lax.all_gather(normed_one, "tp", axis=0, tiled=True)
    query_before_rotation = jnp.dot(full_rows, w_query, preferred_element_type=jnp.float32).reshape(
        seq_len, q_heads, head_size
    )
    keyval_pre = jnp.einsum(
        "sd,dhe->she", full_rows, key_value_weight, preferred_element_type=jnp.float32
    )
    query_vectors = (
        apply_rotation(query_before_rotation, cosine_rows, sine_rows)
        .astype(jnp.bfloat16)
        .reshape(seq_len, kv_heads, heads_per_group, head_size)
    )
    keys_rot = apply_rotation(keyval_pre[:, :, :head_size], cosine_rows, sine_rows).astype(
        jnp.bfloat16
    )
    values = keyval_pre[:, :, head_size:].astype(jnp.bfloat16)
    positions = jnp.arange(seq_len)
    doc_ids = segments[0]
    allowed = (doc_ids[:, None] == doc_ids[None, :]) & (positions[None, :] <= positions[:, None])

    def masked_scores():
        raw_scores = (
            jnp.einsum(
                "qhgd,khd->hgqk", query_vectors, keys_rot, preferred_element_type=jnp.float32
            )
            * score_scale
        )
        return jnp.where(allowed, raw_scores, neg_fill)

    scores = masked_scores()
    peak_score = jnp.max(scores, axis=-1, keepdims=True)
    log_total = peak_score + jnp.log(jnp.sum(jnp.exp(scores - peak_score), axis=-1, keepdims=True))
    probs_low = jnp.exp(scores - log_total).astype(jnp.bfloat16)
    attended = jnp.einsum("hgqk,khd->qhgd", probs_low, values, preferred_element_type=jnp.float32)
    attended = attended.reshape(seq_len, q_heads * head_size).astype(jnp.bfloat16)
    x_mid = x_float + lax.psum_scatter(
        jnp.dot(attended, w_output, preferred_element_type=jnp.float32).astype(jnp.bfloat16),
        "tp",
        scatter_dimension=0,
        tiled=True,
    ).astype(jnp.float32)
    hat_two, factor_two = normalize(x_mid)
    normed_two = (hat_two * moe_gain).astype(jnp.bfloat16)
    logits = jnp.dot(normed_two, w_router, preferred_element_type=jnp.float32)
    chosen_hot = routes[:, :, None] == jnp.arange(expert_count, dtype=jnp.int32)[None, None, :]
    chosen = jnp.sum(jnp.where(chosen_hot, logits[:, None, :], 0.0), axis=-1)
    gate_weights = jax.nn.softmax(chosen, axis=-1)
    route_total = row_count * top_count
    flat_hot = chosen_hot.reshape(route_total, expert_count).astype(jnp.int32)
    earlier = jnp.cumsum(flat_hot, axis=0) - flat_hot
    position = jnp.sum(earlier * flat_hot, axis=1)
    slot_of_route = routes.reshape(route_total) * capacity + position
    route_of_slot = (
        jnp.full((expert_count * capacity,), route_total, jnp.int32)
        .at[slot_of_route]
        .set(jnp.arange(route_total, dtype=jnp.int32))
    )
    padded_rows = jnp.concatenate([normed_two, jnp.zeros((1, width), jnp.bfloat16)], axis=0)
    send_rows = padded_rows[route_of_slot // top_count].reshape(-1, local_experts, capacity, width)
    received = deliver(send_rows)
    source_count = received.shape[0]
    gate_up = jnp.einsum("kxcd,xjfd->kxcjf", received, w_in, preferred_element_type=jnp.float32)
    gate_pre = gate_up[:, :, :, 0]
    up_pre = gate_up[:, :, :, 1]
    active = (jax.nn.silu(gate_pre) * up_pre).astype(jnp.bfloat16)

    def expert_forward(first_row, num_rows):
        return jnp.einsum("kxcf,xfd->kxcd", active, w_out, preferred_element_type=jnp.float32)

    returned = collect(expert_forward, source_count)
    route_rows = returned.reshape(-1, width)[slot_of_route].reshape(row_count, top_count, width)
    expert_mix = jnp.sum(gate_weights[:, :, None] * route_rows, axis=1)
    block_out = (x_mid + expert_mix).astype(jnp.bfloat16)
    grad_out = out_cotangent.astype(jnp.float32)
    grad_gates = jnp.sum(route_rows * grad_out[:, None, :], axis=-1)
    slot_grad = (
        (gate_weights[:, :, None] * grad_out[:, None, :])
        .astype(jnp.bfloat16)
        .reshape(route_total, width)
    )
    slot_grad = jnp.concatenate([slot_grad, jnp.zeros((1, width), jnp.bfloat16)], axis=0)
    grad_received = deliver(slot_grad[route_of_slot].reshape(send_rows.shape))
    grad_active = jnp.einsum(
        "kxcd,xfd->kxcf", grad_received, w_out, preferred_element_type=jnp.float32
    )
    sigmoid_gate = jax.nn.sigmoid(gate_pre)
    grad_gate = grad_active * up_pre * sigmoid_gate * (1.0 + gate_pre * (1.0 - sigmoid_gate))
    grad_up = grad_active * gate_pre * sigmoid_gate
    grad_gate_up = jnp.stack([grad_gate, grad_up], axis=3).astype(jnp.bfloat16)
    grad_w_out = jnp.einsum(
        "kxcf,kxcd->xfd", active, grad_received, preferred_element_type=jnp.float32
    )
    grad_w_in = jnp.einsum(
        "kxcjf,kxcd->xjfd", grad_gate_up, received, preferred_element_type=jnp.float32
    )

    def expert_backward(first_row, num_rows):
        return jnp.einsum(
            "kxcjf,xjfd->kxcd", grad_gate_up, w_in, preferred_element_type=jnp.float32
        )

    grad_slots = collect(expert_backward, source_count)
    grad_routes = grad_slots.reshape(-1, width)[slot_of_route].reshape(row_count, top_count, width)
    mean_grad = jnp.sum(gate_weights * grad_gates, axis=-1, keepdims=True)
    grad_chosen = gate_weights * (grad_gates - mean_grad)
    grad_logits = jnp.sum(jnp.where(chosen_hot, grad_chosen[:, :, None], 0.0), axis=1).astype(
        jnp.bfloat16
    )
    grad_normed_two = jnp.sum(grad_routes, axis=1) + jnp.einsum(
        "re,de->rd", grad_logits, w_router, preferred_element_type=jnp.float32
    )
    grad_w_router = jnp.einsum(
        "rd,re->de", normed_two, grad_logits, preferred_element_type=jnp.float32
    )
    grad_from_moe, grad_moe_gain = norm_back(grad_normed_two, hat_two, factor_two, moe_gain)
    grad_mid = grad_out + grad_from_moe
    grad_full = lax.all_gather(grad_mid.astype(jnp.bfloat16), "tp", axis=0, tiled=True)
    grad_attended = jnp.einsum(
        "sd,ed->se", grad_full, w_output, preferred_element_type=jnp.float32
    ).astype(jnp.bfloat16)
    grad_w_output = jnp.einsum("se,sd->ed", attended, grad_full, preferred_element_type=jnp.float32)
    grad_heads = grad_attended.reshape(seq_len, kv_heads, heads_per_group, head_size)
    probs = jnp.exp(masked_scores() - log_total)
    grad_probs = jnp.einsum(
        "qhgd,khd->hgqk", grad_heads, values, preferred_element_type=jnp.float32
    )
    row_inner = jnp.sum(probs * grad_probs, axis=-1, keepdims=True)
    grad_scores = (probs * (grad_probs - row_inner)).astype(jnp.bfloat16)
    grad_queries = (
        jnp.einsum("hgqk,khd->qhgd", grad_scores, keys_rot, preferred_element_type=jnp.float32)
        * score_scale
    )
    grad_keys = (
        jnp.einsum("hgqk,qhgd->khd", grad_scores, query_vectors, preferred_element_type=jnp.float32)
        * score_scale
    )
    grad_values = jnp.einsum(
        "hgqk,qhgd->khd", probs.astype(jnp.bfloat16), grad_heads, preferred_element_type=jnp.float32
    )
    grad_query_pre = apply_rotation(
        grad_queries.reshape(seq_len, q_heads, head_size), cosine_rows, -sine_rows
    )
    grad_query_pre = grad_query_pre.reshape(seq_len, q_heads * head_size).astype(jnp.bfloat16)
    grad_key_pre = apply_rotation(grad_keys, cosine_rows, -sine_rows)
    grad_keyval_pre = jnp.concatenate([grad_key_pre, grad_values], axis=-1).astype(jnp.bfloat16)
    grad_w_query = jnp.einsum(
        "sd,se->de", full_rows, grad_query_pre, preferred_element_type=jnp.float32
    )
    grad_w_keyval = jnp.einsum(
        "sd,she->dhe", full_rows, grad_keyval_pre, preferred_element_type=jnp.float32
    )
    from_query = jnp.einsum(
        "se,de->sd", grad_query_pre, w_query, preferred_element_type=jnp.float32
    )
    from_keyval = jnp.einsum(
        "she,dhe->sd", grad_keyval_pre, key_value_weight, preferred_element_type=jnp.float32
    )
    grad_normed_one = lax.psum_scatter(
        (from_query + from_keyval).astype(jnp.bfloat16), "tp", scatter_dimension=0, tiled=True
    ).astype(jnp.float32)
    grad_from_attn, grad_attn_gain = norm_back(grad_normed_one, hat_one, factor_one, attn_gain)
    grad_input = grad_mid + grad_from_attn
    grad_w_query, grad_w_keyval, grad_w_output = (
        *sent_together(
            (grad_w_query.astype(jnp.bfloat16), grad_w_keyval.astype(jnp.bfloat16)),
            ("dp", "ep"),
            0,
            1,
        ),
        summed_on_arrival(grad_w_output.astype(jnp.bfloat16), ("dp", "ep"), 1),
    )
    grad_w_in, grad_w_out = (
        lax.psum_scatter(
            grad_w_in.astype(jnp.bfloat16), "dp", scatter_dimension=3, tiled=True
        ).astype(jnp.float32),
        lax.psum_scatter(
            grad_w_out.astype(jnp.bfloat16), "dp", scatter_dimension=2, tiled=True
        ).astype(jnp.float32),
    )
    grad_attn_gain, grad_moe_gain, grad_w_router = lax.psum(
        (grad_attn_gain, grad_moe_gain, grad_w_router), ("dp", "ep", "tp")
    )
    return (
        block_out,
        grad_input,
        grad_attn_gain,
        grad_w_query,
        grad_w_keyval,
        grad_w_output,
        grad_moe_gain,
        grad_w_router,
        grad_w_in,
        grad_w_out,
    )


def solution(mesh):
    return jax.shard_map(
        per_device,
        mesh=mesh,
        in_specs=(
            P(("dp", "ep", "tp"), None),
            P(("dp", "ep"), None),
            P(("dp", "ep", "tp"), None),
            P(),
            P(None, "tp"),
            P(None, "tp", None),
            P("tp", None),
            P(),
            P(),
            P("ep", None, "tp", None),
            P("ep", "tp", None),
            P(("dp", "ep", "tp"), None),
        ),
        out_specs=(
            P(("dp", "ep", "tp"), None),
            P(("dp", "ep", "tp"), None),
            P(),
            P(("dp", "ep"), "tp"),
            P(("dp", "ep"), "tp", None),
            P("tp", ("dp", "ep")),
            P(),
            P(),
            P("ep", None, "tp", "dp"),
            P("ep", "tp", "dp"),
        ),
        check_vma=False,
    )
```

profile of v0, /device:TPU:8, one launch (start us, length us, event | category | flops | bytes accessed | tf_op | source)
XLA Modules:
  0.0 1449.1 jit_solution(4572462817240719823)
XLA Ops:
  15.3 28.0 %all-gather.5.cloned.1.call-done = bf16[512,1536]{1,0:T(8,128)(2,1)} async-done(((bf16[128,1536]{1,0:T(8,128)(2,1)}), bf16[512,1536]{1,0:T(8,128)(2,1)}) %all-gather.5.cloned.1.call-update) | async-done | bytes 1572880 | tf_op jit(solution)/shard_map/all_gather | solution.py:119
  55.2 5.6 reduce-window.6
  61.4 4.3 scatter_custom_fusion
  65.7 20.0 %reduce-scatter.11.cloned.1.call-done = bf16[128,1536]{1,0:T(8,128)(2,1)} async-done(((bf16[512,1536]{1,0:T(8,128)(2,1)}), bf16[128,1536]{1,0:T(8,128)(2,1)}) %reduce-scatter.11.cloned.1.call-update) | async-done | bytes 393232 | tf_op jit(solution)/shard_map/reduce_scatter | solution.py:154
  88.7 5.2 gather_fusion
  93.9 5.3 reshape.322
  99.2 7.8 all_to_all.30
  113.0 10.9 gather_fusion.2
  123.9 5.3 reshape.326
  129.2 7.8 all_to_all.31
  139.2 102.5 %all-gather.7.cloned.1.call-done = bf16[8,10,52,1536]{3,2,0,1:T(8,128)(2,1)} async-done(((bf16[2,10,52,1536]{3,2,0,1:T(8,128)(2,1)}), bf16[8,10,52,1536]{3,2,0,1:T(8,128)(2,1)}) %all-gather.7.cloned.1.call-update) | async-done | bytes 12779536 | tf_op jit(solution)/shard_map/all_gather | solution.py:72
  241.6 15.1 %fusion.28 = f32[8,10,52,2,128]{4,2,3,0,1:T(8,128)} fusion(bf16[10,2,128,1536]{3,2,1,0:T(8,128)(2,1)} %param.21, bf16[8,10,52,1536]{3,2,0,1:T(8,128)(2,1)} %all-gather.7.cloned.1.call-done), kind=kOutput, calls=%fused_computation.61 | convolution fusion | flops 3271557120 | bytes 24903680 | tf_op jit(solution)/shard_map/kxcd,xjfd->kxcjf/dot_general | solution.py:180
  256.7 119.0 %all-gather.9.cloned.1.call-done = bf16[8,10,52,1536]{3,2,0,1:T(8,128)(2,1)} async-done(((bf16[2,10,52,1536]{3,2,0,1:T(8,128)(2,1)}), bf16[8,10,52,1536]{3,2,0,1:T(8,128)(2,1)}) %all-gather.9.cloned.1.call-update) | async-done | bytes 12779536 | tf_op jit(solution)/shard_map/all_gather | solution.py:72
  375.7 12.7 fusion.42
  388.4 9.8 fusion.6
  398.2 7.3 copy.184
  405.5 6.3 copy.128
  411.8 6.8 convert_bitcast_fusion
  420.5 479.7 %all-reduce.11.cloned.1.call-done = (bf16[8,10,52,1536]{3,2,0,1:T(8,128)(2,1)}, bf16[8,10,52,1536]{3,2,0,1:T(8,128)(2,1)}) async-done(((bf16[8,10,52,1536]{3,2,0,1:T(8,128)(2,1)}, bf16[8,10,52,1536]{3,2,0,1:T(8,128)(2,1)}), (bf16[8,10,52,1536]{3,2,0,1:T(8,128)(2,1)}, bf16[8,10,52,1536]{3,2,0,1:T(8,128)(2,1)})) %all-reduce.11.cloned.1.call-update) | async-done | bytes 25559056
  906.9 7.5 all_to_all.32
  914.3 5.6 all-to-all-start.1
  919.9 5.8 reshape.337
  925.7 10.6 gather_fusion.3
  936.3 5.2 bitcast_reduce_fusion
  941.5 5.8 reshape.335
  947.3 10.6 gather_fusion.1
  957.9 5.2 fusion.13
  968.0 9.1 bitcast_convert_fusion.2
  977.2 9.1 copy.171
  986.2 6.8 copy.185
  994.3 12.7 bitcast_convert_fusion.1
  1007.0 20.1 %copy.169 = bf16[10,2,128,1536]{2,1,0,3:T(2,128)(2,1)} copy(bf16[10,2,128,1536]{3,2,1,0:T(8,128)(2,1)} %bitcast_convert_fusion.1) | data formatting | bytes 15728640
  1027.1 17.8 %reshape.399 = bf16[1536,2560]{1,0:T(8,128)(2,1)} reshape(bf16[1536,10,2,128]{3,2,1,0:T(2,128)(2,1)} %bitcast.245) | data formatting | bytes 15728640
  1048.7 5.4 all-to-all-start.5
  1056.7 5.0 fusion.8
  1061.8 2.9 fusion.10
  1075.2 6.7 copy.139
  1087.5 9.4 all-to-all-done.5
  1096.8 7.6 all-to-all-start.4
  1104.5 3.3 reshape.402
  1111.7 164.8 %reduce-scatter.15.cloned.1.call-done = bf16[384,2560]{1,0:T(8,128)(2,1)} async-done(((bf16[1536,2560]{1,0:T(8,128)(2,1)}), bf16[384,2560]{1,0:T(8,128)(2,1)}) %reduce-scatter.15.cloned.1.call-update) | async-done | bytes 1966096
  1276.5 5.1 reshape.400
  1281.6 6.7 copy.170
  1288.4 4.0 convert_element_type.153
  1295.4 14.4 reduce-scatter.13.cloned.1.call-done
  1311.1 39.5 %all-reduce.4 = (f32[1536]{0:T(1024)}, f32[1536]{0:T(1024)}) all-reduce(f32[1536]{0:T(1024)S(1)} %get-tuple-element.14, f32[1536]{0:T(1024)S(1)} %get-tuple-element.12), channel_id=1, replica_groups=mesh['dp'=4,'ep'=2,'tp'=4] {'dp','ep','tp'}, use_global_device_ids=true, to_apply=%region_24.25 | all-reduce | flops 3072 | bytes 24576 | tf_op jit(solution)/shard_map/psum | solution.py:298
  1350.7 3.0 fusion.47
  1357.1 83.4 %all-reduce.9.cloned.1.call-done = f32[1536,20]{0,1:T(8,128)} async-done(((f32[1536,20]{0,1:T(8,128)}), f32[1536,20]{0,1:T(8,128)}) %all-reduce.9.cloned.1.call-update) | async-done | bytes 122896 | tf_op jit(solution)/shard_map/psum | solution.py:298
  (223 shorter events, 80.6 us)
Async XLA Ops:
  7.2 45.2 %copy-start = (bf16[384,1536]{1,0:T(8,128)(2,1)S(1)}, bf16[384,1536]{1,0:T(8,128)(2,1)}, u32[]{:S(2)}) copy-start(bf16[384,1536]{1,0:T(8,128)(2,1)} %param.18) | copy-start | bytes 3538948
  7.2 38.2 %copy-start.22 = (bf16[1536,384]{1,0:T(8,128)(2,1)S(1)}, bf16[1536,384]{1,0:T(8,128)(2,1)}, u32[]{:S(2)}) copy-start(bf16[1536,384]{1,0:T(8,128)(2,1)} %param.16) | copy-start | bytes 3538948
  7.2 36.1 %all-gather.5.cloned.1.call-start = ((), (), s32[]{:S(2)}) async-start(), calls=%async_computation.10 | async-start | bytes 1966080 | tf_op jit(solution)/shard_map/all_gather | solution.py:119
  11.0 74.8 %reduce-scatter.11.cloned.1.call-start = ((), (), s32[]{:S(2)}) async-start(), calls=%async_computation.11 | async-start | bytes 1966080 | tf_op jit(solution)/shard_map/reduce_scatter | solution.py:154
  13.3 34.5 %copy-start.6 = (bf16[1536,2,128]{0,2,1:T(8,128)(2,1)}, bf16[1536,2,128]{0,2,1:T(8,128)(2,1)S(1)}, u32[]{:S(2)}) copy-start(bf16[1536,2,128]{0,2,1:T(8,128)(2,1)S(1)} %copy.113) | copy-start | bytes 2359300
  14.3 33.5 %copy-start.20 = (f32[512,32]{0,1:T(8,128)}, f32[512,32]{0,1:T(8,128)S(1)}, u32[]{:S(2)}) copy-start(f32[512,32]{0,1:T(8,128)S(1)} %get-tuple-element.37) | copy-start | bytes 196612
  15.3 35.3 %copy-start.11 = (pred[512,512]{0,1:T(8,128)(4,1)}, pred[512,512]{0,1:T(8,128)(4,1)S(1)}, u32[]{:S(2)}) copy-start(pred[512,512]{0,1:T(8,128)(4,1)S(1)} %fusion.44) | copy-start | bytes 786436
  45.3 5.2 copy-start.18
  45.4 3.8 copy-start.34
  45.4 3.8 copy-start.36
  49.2 3.2 copy-start.1
  52.4 2.3 copy-start.43
  52.4 33.4 %copy-start.2 = (bf16[128,1536]{1,0:T(8,128)(2,1)S(1)}, bf16[128,1536]{1,0:T(8,128)(2,1)}, u32[]{:S(2)}) copy-start(bf16[128,1536]{1,0:T(8,128)(2,1)} %param.12) | copy-start | bytes 1179652
  52.4 35.1 %copy-start.40 = (f32[1536]{0:T(1024)S(1)}, f32[1536]{0:T(1024)}, u32[]{:S(2)}) copy-start(f32[1536]{0:T(1024)} %param.19) | copy-start | bytes 18436
  54.6 187.0 %all-gather.7.cloned.1.call-start = ((), (), s32[]{:S(2)}) async-start(), calls=%async_computation.12 | async-start | bytes 17203200 | tf_op jit(solution)/shard_map/all_gather | solution.py:72
  88.7 21.5 %copy-start.14 = (bf16[128,1536]{1,0:T(8,128)(2,1)}, bf16[128,1536]{1,0:T(8,128)(2,1)S(1)}, u32[]{:S(2)}) copy-start(bf16[128,1536]{1,0:T(8,128)(2,1)S(1)} %multiply_convert_fusion.1) | copy-start | bytes 1179652
  109.1 266.6 %all-gather.9.cloned.1.call-start = ((), (), s32[]{:S(2)}) async-start(), calls=%async_computation.13 | async-start | bytes 17203200 | tf_op jit(solution)/shard_map/all_gather | solution.py:72
  110.1 2.8 copy-start.10
  110.5 2.5 copy-start.44
  139.1 761.1 %all-reduce.11.cloned.1.call-start = ((), (), s32[]{:S(2)}) async-start(), calls=%async_computation.19 | async-start | bytes 55050240
  388.4 9.8 copy-start.24
  405.5 6.3 copy-start.4
  914.3 27.1 %all-to-all-start.1 = ((bf16[2,10,52,1536]{3,2,1,0:T(8,128)(2,1)}), bf16[2,10,52,1536]{3,2,1,0:T(8,128)(2,1)}, u32[]{:S(2)}, u32[]{:S(2)}) async-start(bf16[2,10,52,1536]{3,2,1,0:T(8,128)(2,1)} %copy.123), calls=%async_computation.2 | async-start | bytes 6881280 | tf_op jit(solution)/shard_map/all_to_all | solution.py:84
  919.9 125.1 %all-gather.11.cloned.1.call-start = ((), (), s32[]{:S(2)}) async-start(), calls=%async_computation.14 | async-start | bytes 1966080 | tf_op jit(solution)/shard_map/all_gather | solution.py:235
  957.8 5.3 copy-start.45
  957.8 5.4 copy-start.3
  957.8 5.4 copy-start.5
  957.8 5.5 copy-start.33
  957.8 5.5 copy-start.41
  957.9 5.5 copy-start.47
  968.0 136.5 %reduce-scatter.17.cloned.1.call-start = ((), (), s32[]{:S(2)}) async-start(), calls=%async_computation.18 | async-start | bytes 4915200
  993.0 283.5 %reduce-scatter.15.cloned.1.call-start = ((), (), s32[]{:S(2)}) async-start(), calls=%async_computation.17 | async-start | bytes 9830400
  1048.7 48.1 %all-to-all-start.5 = ((bf16[8,384,192]{1,2,0:T(8,128)(2,1)}), bf16[8,384,192]{1,2,0:T(8,128)(2,1)}, u32[]{:S(2)}, u32[]{:S(2)}) async-start(bf16[8,384,192]{1,2,0:T(8,128)(2,1)} %bitcast.56), calls=%async_computation.7 | async-start | bytes 2359296 | tf_op jit(solution)/shard_map/all_to_all | solution.py:21
  1054.1 2.5 copy-start.39
  1054.1 255.6 %reduce-scatter.13.cloned.1.call-start = ((), (), s32[]{:S(2)}) async-start(), calls=%async_computation.15 | async-start | bytes 1966080 | tf_op jit(solution)/shard_map/reduce_scatter | solution.py:276
  1054.3 2.3 copy-start.12
  1054.3 2.3 copy-start.19
  1056.6 5.1 copy-start.30
  1056.6 5.1 slice-start
  1056.7 5.1 slice-start.1
  1064.7 2.3 copy-start.35
  1083.4 2.5 copy-start.17
  1096.8 256.8 %all-to-all-start.4 = ((bf16[8,192,640]{2,1,0:T(8,128)(2,1)}), bf16[8,192,640]{2,1,0:T(8,128)(2,1)}, u32[]{:S(2)}, u32[]{:S(2)}) async-start(bf16[8,192,640]{2,1,0:T(8,128)(2,1)} %pad_maximum_fusion.1), calls=%async_computation.6 | async-start | bytes 3932160 | tf_op jit(solution)/shard_map/all_to_all | solution.py:21
  1104.5 336.0 %all-reduce.9.cloned.1.call-start = ((), (), s32[]{:S(2)}) async-start(), calls=%async_computation.16 | async-start | bytes 294912 | tf_op jit(solution)/shard_map/psum | solution.py:298
  1288.4 4.0 copy-start.15
  1288.4 21.4 %copy-start.42 = (f32[1536]{0:T(1024)S(1)}, f32[1536]{0:T(1024)}, u32[]{:S(2)}) copy-start(f32[1536]{0:T(1024)} %param.15) | copy-start | bytes 18436
  1288.4 21.4 %copy-start.49 = (f32[128]{0:T(128)S(1)}, f32[128]{0:T(128)}, u32[]{:S(2)}) copy-start(f32[128]{0:T(128)} %copy-done.48) | copy-start | bytes 1540
  1288.4 62.3 %copy-start.9 = (f32[128,1536]{1,0:T(8,128)S(1)}, f32[128,1536]{1,0:T(8,128)}, u32[]{:S(2)}) copy-start(f32[128,1536]{1,0:T(8,128)} %copy-done.8) | copy-start | bytes 2359300
  (18 other events, 24.2 us)
Sparse Core Ops, SparseCore 0:
  11.1 32.1 all-gather.4
  54.7 31.0 reduce-scatter.10
  109.2 132.3 all-gather.6
  243.3 132.3 all-gather.8
  418.7 481.3 all-reduce.10
  968.1 31.0 all-gather.10
  1002.2 93.7 reduce-scatter.16
  1098.4 178.0 reduce-scatter.14
  1279.8 29.9 reduce-scatter.12
  1316.7 123.7 all-reduce.8
where the time goes:
time: 1460 us; the launch traced here: 1450 us
  waiting for transfers between devices  1020 us (70%)
  local copies, waits for them, and re-layouts  183 us (13%)
  matrix products  99.9 us (7%)
  blocking collectives  62.6 us (4%)
  other arithmetic  46.5 us (3%)
  starting transfers between devices  19.7 us (1%)
  between operations  16 us (1%)
    unnamed x13, waiting for transfers between devices  645 us
    all_gather x2, waiting for transfers between devices, deliver(): return lax.all_gather(arrived, 'tp', axis=0, tiled=True)  221 us
    unnamed x122, local copies, waits for them, and re-layouts  85.5 us
    psum x1, waiting for transfers between devices, per_device(): lax.psum((grad_attn_gain, grad_moe_gain, grad_w_router), ('dp', 'ep', 'tp'))  83.4 us
    psum x1, blocking collectives, per_device(): lax.psum((grad_attn_gain, grad_moe_gain, grad_w_router), ('dp', 'ep', 'tp'))  39.5 us
  transfers between devices with their start and end apart: 13, of which 9 were waited for; matrix products, arithmetic and copies ran while one was open for 15% of the time, Pallas kernels for 0%

commit v1 on v0

v1 whole, which is shorter than its diff:
```python
import functools
import math

import jax
import jax.numpy as jnp
from jax import lax
from jax.experimental import pallas as pl
from jax.experimental.pallas import tpu as pltpu
from jax.sharding import PartitionSpec as P

eps_norm = 1e-05
rope_base = 10000.0
neg_fill = -1000000000.0
MESH = pl.DeviceIdType.MESH
bf16 = jnp.bfloat16
f32 = jnp.float32


def greet(partners):
    barrier = pltpu.get_barrier_semaphore()
    for partner in partners:
        pl.semaphore_signal(barrier, inc=1, device_id=partner, device_id_type=MESH)
    pl.semaphore_wait(barrier, len(partners))


def rows_at(start, count):
    return pl.ds(pl.multiple_of(start, count), count)


def gather_kernel(with_ep, block_ref, whole_ref, local_sem, send_sem, recv_sem):
    rows = block_ref.shape[0]
    half = rows // 2
    t, e = lax.axis_index("tp"), lax.axis_index("ep")
    near, far = {"tp": t ^ 1}, {"tp": t ^ 2}
    twin = {"ep": 1 - e}
    greet((near, far, twin) if with_ep else (near, far))
    tp = lax.axis_size("tp")
    base = e * (tp * rows) if with_ep else 0

    def place(tt, part, count):
        return whole_ref.at[rows_at(base + tt * rows + part * half, count)]

    def send(src, dst, k, device):
        copy = pltpu.make_async_remote_copy(
            src, dst, send_sem.at[k], recv_sem.at[k], device_id=device, device_id_type=MESH
        )
        copy.start()
        return copy

    def own(part):
        return block_ref.at[pl.ds(part * half, half)]

    local = pltpu.make_async_copy(block_ref, place(t, 0, rows), local_sem)
    near_a = send(own(0), place(t, 0, half), 0, near)
    far_b = send(own(1), place(t, 1, half), 1, far)
    near_b = send(own(1), place(t, 1, half), 2, near)
    far_a = send(own(0), place(t, 0, half), 3, far)
    local.start()
    copies = [near_a, far_b, near_b, far_a]
    if with_ep:
        twin_own = send(block_ref, place(t, 0, rows), 6, twin)
        copies.append(twin_own)
    near_a.wait_recv()
    on_a = send(place(t ^ 1, 0, half), place(t ^ 1, 0, half), 4, far)
    far_b.wait_recv()
    on_b = send(place(t ^ 2, 1, half), place(t ^ 2, 1, half), 5, near)
    near_b.wait_recv()
    far_a.wait_recv()
    if with_ep:
        twin_near = send(place(t ^ 1, 0, rows), place(t ^ 1, 0, rows), 7, twin)
        twin_far = send(place(t ^ 2, 0, rows), place(t ^ 2, 0, rows), 8, twin)
    on_a.wait_recv()
    on_b.wait_recv()
    if with_ep:
        twin_diag = send(place(t ^ 3, 0, rows), place(t ^ 3, 0, rows), 9, twin)
        for copy in (twin_own, twin_near, twin_far, twin_diag):
            copy.wait_recv()
        copies += [twin_near, twin_far, twin_diag]
    local.wait()
    for copy in copies + [on_a, on_b]:
        copy.wait_send()


def gather(block, with_ep, collective_id):
    rows, width = block.shape
    count = lax.axis_size("tp") * (lax.axis_size("ep") if with_ep else 1)
    return pl.pallas_call(
        functools.partial(gather_kernel, with_ep),
        out_shape=jax.ShapeDtypeStruct((count * rows, width), block.dtype),
        in_specs=[pl.BlockSpec(memory_space=pl.ANY)],
        out_specs=pl.BlockSpec(memory_space=pl.ANY),
        scratch_shapes=[
            pltpu.SemaphoreType.DMA,
            pltpu.SemaphoreType.DMA((10,)),
            pltpu.SemaphoreType.DMA((10,)),
        ],
        name="gather_plane" if with_ep else "gather_tp",
        cost_estimate=pl.CostEstimate(flops=0, bytes_accessed=40 * 10**6, transcendentals=0),
        compiler_params=pltpu.CompilerParams(
            collective_id=collective_id, has_side_effects=True, vmem_limit_bytes=16 * 2**20
        ),
    )(block)


def scatter_kernel(with_ep, part_ref, sum_ref, mine, twins, arrived, passed, local_sem, send_sem, recv_sem):
    rows = sum_ref.shape[0]
    half = rows // 2
    t, e = lax.axis_index("tp"), lax.axis_index("ep")
    tp = lax.axis_size("tp")
    near, far = {"tp": t ^ 1}, {"tp": t ^ 2}
    twin = {"ep": 1 - e}
    greet((near, far, twin) if with_ep else (near, far))
    base = e * (tp * rows) if with_ep else 0
    other = (1 - e) * (tp * rows)

    def send(src, dst, k, device):
        copy = pltpu.make_async_remote_copy(
            src, dst, send_sem.at[k], recv_sem.at[k], device_id=device, device_id_type=MESH
        )
        copy.start()
        return copy

    order = (3, 1, 2, 0)
    locals_, twin_copies = {}, {}
    for k in order:
        if with_ep:
            twin_copies[k] = send(
                part_ref.at[rows_at(other + (t ^ k) * rows, rows)], twins.at[k], k, twin
            )
        locals_[k] = pltpu.make_async_copy(
            part_ref.at[rows_at(base + (t ^ k) * rows, rows)], mine.at[k], local_sem.at[k]
        )
        locals_[k].start()

    def ready(k):
        locals_[k].wait()
        if with_ep:
            twin_copies[k].wait_recv()
            mine[k] = (mine[k].astype(f32) + twins[k].astype(f32)).astype(mine.dtype)

    first, second = pl.ds(0, half), pl.ds(half, half)
    ready(3)
    a_on = send(mine.at[3, first], arrived.at[0, 0], 4, near)
    b_on = send(mine.at[3, second], arrived.at[1, 0], 5, far)
    ready(1)
    a_own = send(mine.at[1, first], arrived.at[0, 1], 6, near)
    ready(2)
    b_own = send(mine.at[2, second], arrived.at[1, 1], 7, far)
    ready(0)
    a_on.wait_recv()
    mine[2, first] = (mine[2, first].astype(f32) + arrived[0, 0].astype(f32)).astype(mine.dtype)
    a_last = send(mine.at[2, first], passed.at[0], 8, far)
    b_on.wait_recv()
    mine[1, second] = (mine[1, second].astype(f32) + arrived[1, 0].astype(f32)).astype(mine.dtype)
    b_last = send(mine.at[1, second], passed.at[1], 9, near)
    a_own.wait_recv()
    b_own.wait_recv()
    a_last.wait_recv()
    sum_ref[first] = (
        mine[0, first].astype(f32) + arrived[0, 1].astype(f32) + passed[0].astype(f32)
    ).astype(sum_ref.dtype)
    b_last.wait_recv()
    sum_ref[second] = (
        mine[0, second].astype(f32) + arrived[1, 1].astype(f32) + passed[1].astype(f32)
    ).astype(sum_ref.dtype)
    copies = [a_on, b_on, a_own, b_own, a_last, b_last]
    if with_ep:
        copies += list(twin_copies.values())
    for copy in copies:
        copy.wait_send()


def scatter_sum(parts, with_ep, collective_id):
    count = lax.axis_size("tp") * (lax.axis_size("ep") if with_ep else 1)
    rows, width = parts.shape[0] // count, parts.shape[1]
    return pl.pallas_call(
        functools.partial(scatter_kernel, with_ep),
        out_shape=jax.ShapeDtypeStruct((rows, width), f32),
        in_specs=[pl.BlockSpec(memory_space=pl.ANY)],
        out_specs=pl.BlockSpec(memory_space=pltpu.VMEM),
        scratch_shapes=[
            pltpu.VMEM((4, rows, width), bf16),
            pltpu.VMEM((4, rows, width) if with_ep else (4, 16, 128), bf16),
            pltpu.VMEM((2, 2, rows // 2, width), bf16),
            pltpu.VMEM((2, rows // 2, width), bf16),
            pltpu.SemaphoreType.DMA((4,)),
            pltpu.SemaphoreType.DMA((10,)),
            pltpu.SemaphoreType.DMA((10,)),
        ],
        name="scatter_plane" if with_ep else "scatter_tp",
        cost_estimate=pl.CostEstimate(flops=0, bytes_accessed=40 * 10**6, transcendentals=0),
        compiler_params=pltpu.CompilerParams(
            collective_id=collective_id, has_side_effects=True, vmem_limit_bytes=24 * 2**20
        ),
    )(parts)


def halved_over_dp(blocks):
    dp = lax.axis_size("dp")
    d = lax.axis_index("dp")
    if dp & (dp - 1):
        return lax.psum_scatter(blocks, "dp", scatter_dimension=0, tiled=False).astype(f32)
    step = 1
    while step < dp:
        bit = (d // step) % 2
        pairs = blocks.reshape(-1, 2, *blocks.shape[1:])
        kept = lax.dynamic_index_in_dim(pairs, bit, 1, keepdims=False)
        given = lax.dynamic_index_in_dim(pairs, 1 - bit, 1, keepdims=False)
        got = lax.ppermute(given, "dp", [(i, i ^ step) for i in range(dp)])
        total = kept.astype(f32) + got.astype(f32)
        step *= 2
        blocks = total if step == dp else total.astype(bf16)
    return blocks[0]


def rope_tables(length, head_size):
    half_size = head_size // 2
    frequency = jnp.exp(
        jnp.arange(half_size, dtype=f32) * (-2.0 * math.log(rope_base) / head_size)
    )
    angles = jnp.arange(length, dtype=f32)[:, None] * frequency[None, :]
    return (jnp.cos(angles)[:, None, :], jnp.sin(angles)[:, None, :])


def apply_rotation(tensor, cosine_rows, sine_rows):
    half_size = tensor.shape[-1] // 2
    first = tensor[..., :half_size]
    second = tensor[..., half_size:]
    return jnp.concatenate(
        [first * cosine_rows - second * sine_rows, second * cosine_rows + first * sine_rows],
        axis=-1,
    )


def normalize(matrix):
    factor = lax.rsqrt(jnp.mean(matrix * matrix, axis=-1, keepdims=True) + eps_norm)
    return (matrix * factor, factor)


def norm_back(grad_normed, normed_hat, factor, gain):
    grad_hat = grad_normed * gain
    grad_inner = jnp.mean(grad_hat * normed_hat, axis=-1, keepdims=True)
    return (
        factor * (grad_hat - normed_hat * grad_inner),
        jnp.sum(grad_normed * normed_hat, axis=0),
    )


def dot(a, b, dims):
    return lax.dot_general(a, b, ((dims[:1], dims[1:]), ((), ())), preferred_element_type=f32)


def per_device(
    activations,
    segments,
    routes,
    attn_gain,
    w_query,
    key_value_weight,
    w_output,
    moe_gain,
    w_router,
    w_in,
    w_out,
    out_cotangent,
):
    row_count, width = activations.shape
    tp_count = lax.axis_size("tp")
    ep_count = lax.axis_size("ep")
    dp_count = lax.axis_size("dp")
    e_index = lax.axis_index("ep")
    seq_len = row_count * tp_count
    head_size = key_value_weight.shape[2] // 2
    kv_heads = key_value_weight.shape[1]
    q_heads = w_query.shape[1] // head_size
    heads_per_group = q_heads // kv_heads
    top_count = routes.shape[1]
    expert_count = w_router.shape[1]
    local_experts = w_in.shape[0]
    hidden = w_in.shape[2]
    score_scale = 1.0 / math.sqrt(head_size)

    routes_low = jnp.pad(routes.astype(bf16), ((0, 0), (0, 128 - top_count)), constant_values=255)
    plane_grad = lax.all_gather(
        jnp.concatenate([out_cotangent, routes_low], axis=1), ("ep", "tp"), axis=0, tiled=True
    )
    grad_rows = plane_grad[:, :width]
    plane_routes = plane_grad[:, width : width + top_count].astype(jnp.int32)

    cosine_rows, sine_rows = rope_tables(seq_len, head_size)
    x_float = activations.astype(f32)
    hat_one, factor_one = normalize(x_float)
    full_x = gather(activations, False, 0)
    full_rows = (normalize(full_x.astype(f32))[0] * attn_gain).astype(bf16)
    query_before_rotation = jnp.dot(full_rows, w_query, preferred_element_type=f32).reshape(
        seq_len, q_heads, head_size
    )
    keyval_pre = jnp.einsum("sd,dhe->she", full_rows, key_value_weight, preferred_element_type=f32)
    query_vectors = (
        apply_rotation(query_before_rotation, cosine_rows, sine_rows)
        .astype(bf16)
        .reshape(seq_len, kv_heads, heads_per_group, head_size)
    )
    keys_rot = apply_rotation(keyval_pre[:, :, :head_size], cosine_rows, sine_rows).astype(bf16)
    values = keyval_pre[:, :, head_size:].astype(bf16)
    positions = jnp.arange(seq_len)
    doc_ids = segments[0]
    allowed = (doc_ids[:, None] == doc_ids[None, :]) & (positions[None, :] <= positions[:, None])

    def masked_scores():
        raw_scores = (
            jnp.einsum("qhgd,khd->hgqk", query_vectors, keys_rot, preferred_element_type=f32)
            * score_scale
        )
        return jnp.where(allowed, raw_scores, neg_fill)

    scores = masked_scores()
    peak_score = jnp.max(scores, axis=-1, keepdims=True)
    log_total = peak_score + jnp.log(jnp.sum(jnp.exp(scores - peak_score), axis=-1, keepdims=True))
    probs_low = jnp.exp(scores - log_total).astype(bf16)
    attended = jnp.einsum("hgqk,khd->qhgd", probs_low, values, preferred_element_type=f32)
    attended = attended.reshape(seq_len, q_heads * head_size).astype(bf16)
    x_mid = x_float + scatter_sum(
        jnp.dot(attended, w_output, preferred_element_type=f32).astype(bf16), False, 1
    )
    hat_two, factor_two = normalize(x_mid)
    normed_two = (hat_two * moe_gain).astype(bf16)
    rows_two = gather(normed_two, True, 2)

    logits = jnp.dot(rows_two, w_router, preferred_element_type=f32)
    experts = jnp.arange(expert_count, dtype=jnp.int32)
    used = jnp.any(plane_routes[:, :, None] == experts[None, None, :], axis=1)
    peak = jnp.max(jnp.where(used, logits, -jnp.inf), axis=-1, keepdims=True)
    weight = jnp.where(used, jnp.exp(jnp.where(used, logits - peak, 0.0)), 0.0)
    gates = weight / jnp.sum(weight, axis=-1, keepdims=True)
    local_gates = lax.dynamic_slice_in_dim(gates, e_index * local_experts, local_experts, 1)

    group = 2 if local_experts % 2 == 0 else 1
    tokens = rows_two.shape[0]
    mixed_all, grad_all, gate_terms, weight_grads = [], [], [], []
    for start in range(0, local_experts, group):
        now = slice(start, start + group)
        into = w_in[now].reshape(group * 2 * hidden, width)
        out_of = w_out[now].reshape(group * hidden, width)
        gate_up = dot(rows_two, into, (1, 1)).reshape(tokens, group, 2, hidden)
        gate_pre, up_pre = gate_up[:, :, 0], gate_up[:, :, 1]
        back = dot(grad_rows, out_of, (1, 1)).reshape(tokens, group, hidden)
        g = local_gates[:, now][:, :, None]
        sig = jax.nn.sigmoid(gate_pre)
        silu = gate_pre * sig
        active = silu * up_pre
        gate_terms.append(jnp.sum(active * back, axis=-1))
        mixed = (g * active).astype(bf16).reshape(tokens, group * hidden)
        grad_active = g * back
        grad_gate = grad_active * up_pre * sig * (1.0 + gate_pre * (1.0 - sig))
        grad_up = grad_active * silu
        grad_gate_up = (
            jnp.stack([grad_gate, grad_up], axis=2)
            .astype(bf16)
            .reshape(tokens, group * 2 * hidden)
        )
        mixed_all.append(mixed)
        grad_all.append(grad_gate_up)
        columns = width // dp_count
        grad_in = jnp.einsum(
            "tk,tcd->ckd",
            grad_gate_up,
            rows_two.reshape(tokens, dp_count, columns),
            preferred_element_type=f32,
        ).astype(bf16)
        grad_out = jnp.einsum(
            "tk,tcd->ckd",
            mixed,
            grad_rows.reshape(tokens, dp_count, columns),
            preferred_element_type=f32,
        ).astype(bf16)
        weight_grads.append(halved_over_dp(jnp.concatenate([grad_in, grad_out], axis=1)))
    mixed_all = jnp.concatenate(mixed_all, axis=1)
    grad_all = jnp.concatenate(grad_all, axis=1)
    local_terms = jnp.concatenate(gate_terms, axis=1)

    local_inner = jnp.sum(local_gates * local_terms, axis=-1, keepdims=True)
    all_terms = lax.dynamic_update_slice_in_dim(
        jnp.zeros_like(gates), local_terms, e_index * local_experts, 1
    )
    grad_logits = gates * (all_terms - local_inner)
    logits_high = grad_logits.astype(bf16)
    logits_rest = (grad_logits - logits_high.astype(f32)).astype(bf16)
    grad_rows_two = (
        dot(grad_all, w_in.reshape(-1, width), (1, 0))
        + dot(logits_high, w_router, (1, 1))
        + dot(logits_rest, w_router, (1, 1))
    )
    grad_w_router = dot(rows_two, logits_high, (0, 0)) + dot(rows_two, logits_rest, (0, 0))

    grad_normed_two = scatter_sum(grad_rows_two.astype(bf16), True, 3)
    grad_out = out_cotangent.astype(f32)
    grad_from_moe, grad_moe_gain = norm_back(grad_normed_two, hat_two, factor_two, moe_gain)
    grad_mid = grad_out + grad_from_moe
    grad_full = gather(grad_mid.astype(bf16), False, 4)
    expert_mix = scatter_sum(dot(mixed_all, w_out.reshape(-1, width), (1, 0)).astype(bf16), True, 5)
    block_out = (x_mid + expert_mix).astype(bf16)

    grad_attended = dot(grad_full, w_output, (1, 1)).astype(bf16)
    grad_w_output = dot(grad_full, attended, (0, 0)).astype(bf16)
    grad_heads = grad_attended.reshape(seq_len, kv_heads, heads_per_group, head_size)
    probs = jnp.exp(masked_scores() - log_total)
    grad_probs = jnp.einsum("qhgd,khd->hgqk", grad_heads, values, preferred_element_type=f32)
    row_inner = jnp.sum(probs * grad_probs, axis=-1, keepdims=True)
    grad_scores = (probs * (grad_probs - row_inner)).astype(bf16)
    grad_queries = (
        jnp.einsum("hgqk,khd->qhgd", grad_scores, keys_rot, preferred_element_type=f32)
        * score_scale
    )
    grad_keys = (
        jnp.einsum("hgqk,qhgd->khd", grad_scores, query_vectors, preferred_element_type=f32)
        * score_scale
    )
    grad_values = jnp.einsum(
        "hgqk,qhgd->khd", probs.astype(bf16), grad_heads, preferred_element_type=f32
    )
    grad_query_pre = apply_rotation(
        grad_queries.reshape(seq_len, q_heads, head_size), cosine_rows, -sine_rows
    )
    grad_query_pre = grad_query_pre.reshape(seq_len, q_heads * head_size).astype(bf16)
    grad_key_pre = apply_rotation(grad_keys, cosine_rows, -sine_rows)
    grad_keyval_pre = jnp.concatenate([grad_key_pre, grad_values], axis=-1).astype(bf16)
    grad_keyval_flat = grad_keyval_pre.reshape(seq_len, kv_heads * 2 * head_size)
    keyval_flat = key_value_weight.reshape(width, kv_heads * 2 * head_size)
    from_heads = dot(grad_query_pre, w_query, (1, 1)) + dot(grad_keyval_flat, keyval_flat, (1, 1))
    grad_normed_one = scatter_sum(from_heads.astype(bf16), False, 6)
    grad_w_query = dot(full_rows, grad_query_pre, (0, 0)).astype(bf16)
    grad_w_keyval = dot(full_rows, grad_keyval_flat, (0, 0)).astype(bf16)
    grad_from_attn, grad_attn_gain = norm_back(grad_normed_one, hat_one, factor_one, attn_gain)
    grad_input = grad_mid + grad_from_attn

    def over_dp_ep(matrix):
        blocks = matrix.reshape(dp_count, ep_count, -1, matrix.shape[1])
        kept = lax.dynamic_index_in_dim(blocks, e_index, 1, keepdims=False)
        given = lax.dynamic_index_in_dim(blocks, 1 - e_index, 1, keepdims=False)
        got = lax.ppermute(given, "ep", [(0, 1), (1, 0)])
        return halved_over_dp((kept.astype(f32) + got.astype(f32)).astype(bf16))

    grad_w_output = over_dp_ep(grad_w_output).T
    both = over_dp_ep(jnp.concatenate([grad_w_query, grad_w_keyval], axis=1))
    grad_w_query = both[:, : q_heads * head_size]
    grad_w_keyval = both[:, q_heads * head_size :].reshape(-1, kv_heads, 2 * head_size)

    summed = jnp.stack(weight_grads)
    grad_w_in = summed[:, : group * 2 * hidden].reshape(local_experts, 2, hidden, -1)
    grad_w_out = summed[:, group * 2 * hidden :].reshape(local_experts, hidden, -1)
    grad_attn_gain, grad_moe_gain, grad_w_router = lax.psum(
        (grad_attn_gain, grad_moe_gain, grad_w_router), ("dp", "ep", "tp")
    )
    return (
        block_out,
        grad_input,
        grad_attn_gain,
        grad_w_query,
        grad_w_keyval,
        grad_w_output,
        grad_moe_gain,
        grad_w_router,
        grad_w_in,
        grad_w_out,
    )


def solution(mesh):
    return jax.shard_map(
        per_device,
        mesh=mesh,
        in_specs=(
            P(("dp", "ep", "tp"), None),
            P(("dp", "ep"), None),
            P(("dp", "ep", "tp"), None),
            P(),
            P(None, "tp"),
            P(None, "tp", None),
            P("tp", None),
            P(),
            P(),
            P("ep", None, "tp", None),
            P("ep", "tp", None),
            P(("dp", "ep", "tp"), None),
        ),
        out_specs=(
            P(("dp", "ep", "tp"), None),
            P(("dp", "ep", "tp"), None),
            P(),
            P(("dp", "ep"), "tp"),
            P(("dp", "ep"), "tp", None),
            P("tp", ("dp", "ep")),
            P(),
            P(),
            P("ep", None, "tp", "dp"),
            P("ep", "tp", "dp"),
        ),
        check_vma=False,
    )
```

time: 1460 us -> 579 us (0.40)
  waiting for transfers between devices: 1020 us -> 140 us
  Pallas kernels: 0 us -> 121 us
  local copies, waits for them, and re-layouts: 183 us -> 81.1 us
    unnamed x13 -> x2, waiting for transfers between devices: 645 us -> 0.03 us
    all_gather x4 -> x1, waiting for transfers between devices: 250 us -> 0.01 us  [per_device(): lax.all_gather(jnp.concatenate([out_cotangent, routes_low], axis=1), ('ep...]
    ppermute x0 -> x16, waiting for transfers between devices: none -> 140 us  [the longest x14 140 us: halved_over_dp(): got = lax.ppermute(given, 'dp', [(i, i ^ step) for i in range(dp)])]
    pallas_call x0 -> x7, Pallas kernels: none -> 121 us  [the longest x4 68 us: scatter_sum(): pl.pallas_call(functools.partial(scatter_kernel, with_ep), out_shape=jax....]
    psum x1, waiting for transfers between devices: 83.4 us -> 0.01 us  [per_device(): lax.psum((grad_attn_gain, grad_moe_gain, grad_w_router), ('dp', 'ep', 'tp'))]
    unnamed x122 -> x277, local copies, waits for them, and re-layouts: 85.5 us -> 34.3 us
    gather x4 -> x0, local copies, waits for them, and re-layouts: 37.2 us -> none  [the longest x1 10.9 us: per_device(): grad_received = deliver(slot_grad[route_of_slot].reshape(send_rows.shape))]
    reduce_scatter x2 -> x0, waiting for transfers between devices: 34.4 us -> none  [the longest x1 20 us: per_device(): lax.psum_scatter(jnp.dot(attended, w_output, preferred_element_type=jnp.f...]
  transfers between devices with their start and end apart: 13 -> 18, of which waited for: 9 -> 4; matrix products, arithmetic and copies ran while one was open for 15% -> 20% of each run, Pallas kernels for 0% -> 16%
where the time goes in v1:
time: 579 us; the launch traced here: 567 us
  waiting for transfers between devices  140 us (24%)
  Pallas kernels  121 us (21%)
  matrix products  94.3 us (16%)
  local copies, waits for them, and re-layouts  81.1 us (14%)
  blocking collectives  53.3 us (9%)
  other arithmetic  41.4 us (7%)
  starting transfers between devices  19.4 us (3%)
  between operations  16.3 us (3%)
    ppermute x14, waiting for transfers between devices, halved_over_dp(): got = lax.ppermute(given, 'dp', [(i, i ^ step) for i in range(dp)])  140 us
    pallas_call x4, Pallas kernels, scatter_sum(): pl.pallas_call(functools.partial(scatter_kernel, with_ep), out_shape=jax....  68 us
    dot_general x22, matrix products, dot(): lax.dot_general(a, b, ((dims[:1], dims[1:]), ((), ())), preferred_element...  55.3 us
    pallas_call x3, Pallas kernels, gather(): pl.pallas_call(functools.partial(gather_kernel, with_ep), out_shape=jax.S...  53.3 us
    psum x1, blocking collectives, per_device(): lax.psum((grad_attn_gain, grad_moe_gain, grad_w_router), ('dp', 'ep', 'tp'))  53.3 us
    unnamed x277, local copies, waits for them, and re-layouts  34.3 us
    ppermute x14, starting transfers between devices, halved_over_dp(): got = lax.ppermute(given, 'dp', [(i, i ^ step) for i in range(dp)])  18.8 us
  transfers between devices with their start and end apart: 18, of which 4 were waited for; matrix products, arithmetic and copies ran while one was open for 20% of the time, Pallas kernels for 16%

profile of v1, /device:TPU:8, one launch (start us, length us, event | category | flops | bytes accessed | tf_op | source)
XLA Modules:
  0.0 567.1 jit_solution(14815078434065270623)
XLA Ops:
  11.5 2.3 copy.161
  13.8 20.9 %gather_tp.2 = bf16[512,1536]{1,0:T(8,128)(2,1)S(1)} custom-call(bf16[128,1536]{1,0:T(8,128)(2,1)S(1)} %copy-done.7), custom_call_target="tpu_custom_call" | custom-call | bytes 40000000 | tf_op jit(solution)/shard_map/gather_tp/pallas_call | solution.py:87
  44.3 16.4 %scatter_tp.2 = f32[128,1536]{1,0:T(8,128)S(1)} custom-call(bf16[512,1536]{1,0:T(8,128)(2,1)S(1)} %convolution_convert_fusion.1.part_ref), custom_call_target="tpu_custom_call" | custom-call | bytes 40000000 | tf_op jit(solution)/shard_map/scatter_tp/pallas_call | solution.py:176
  61.7 17.1 %gather_plane.1 = bf16[1024,1536]{1,0:T(8,128)(2,1)S(1)} custom-call(bf16[128,1536]{1,0:T(8,128)(2,1)S(1)} %multiply_convert_fusion.5.block_ref), custom_call_target="tpu_custom_call" | custom-call | bytes 40000000 | tf_op jit(solution)/shard_map/gather_plane/pallas_call | solution.py:87
  80.4 4.8 copy.264
  85.3 3.4 fusion.163
  105.2 3.2 fusion.8
  112.4 3.0 select_reduce_fusion
  115.6 4.6 multiply_convert_fusion
  121.1 2.3 multiply_convert_fusion.1
  123.4 2.3 multiply_convert_fusion.2
  125.7 2.8 multiply_convert_fusion.3
  128.4 2.3 multiply_convert_fusion.4
  131.4 2.4 fusion.171
  149.5 2.7 copy-done.99
  153.7 10.5 %fusion.169 = f32[1024,1536]{1,0:T(8,128)S(1)} fusion(bf16[1024,2560]{0,1:T(8,128)(2,1)} %copy-done.99, bf16[2560,1536]{1,0:T(8,128)(2,1)S(1)} %bitcast.618), kind=kOutput, calls=%fused_computation.342 | convolution fusion | flops 8053063680 | bytes 19398656 | tf_op jit(solution)/shard_map/dot_general | solution.py:250
  165.3 17.7 %scatter_plane.3 = f32[128,1536]{1,0:T(8,128)S(1)} custom-call(bf16[1024,1536]{1,0:T(8,128)(2,1)S(1)} %add_convert_fusion.part_ref), custom_call_target="tpu_custom_call" | custom-call | bytes 40000000 | tf_op jit(solution)/shard_map/scatter_plane/pallas_call | solution.py:176
  184.4 15.4 %gather_tp.3 = bf16[512,1536]{1,0:T(8,128)(2,1)S(1)} custom-call(bf16[128,1536]{1,0:T(8,128)(2,1)S(1)} %fusion.150.block_ref), custom_call_target="tpu_custom_call" | custom-call | bytes 40000000 | tf_op jit(solution)/shard_map/gather_tp/pallas_call | solution.py:87
  200.8 2.0 convolution_convert_fusion.3
  204.6 4.6 fusion
  209.2 4.7 fusion.2
  217.4 2.3 convolution_bitcast_fusion
  220.7 1.9 fusion.49
  222.6 1.9 fusion.48
  224.5 1.9 fusion.47
  226.4 2.4 fusion.46
  228.8 1.9 fusion.45
  232.0 2.0 constant_dynamic-update-slice_fusion.4
  238.0 4.6 convolution_convert_fusion.part_ref
  242.6 17.4 %scatter_plane.2 = f32[128,1536]{1,0:T(8,128)S(1)} custom-call(bf16[1024,1536]{1,0:T(8,128)(2,1)S(1)} %convolution_convert_fusion.part_ref), custom_call_target="tpu_custom_call" | custom-call | bytes 40000000 | tf_op jit(solution)/shard_map/scatter_plane/pallas_call | solution.py:176
  260.0 1.8 fusion.40
  272.3 3.0 fusion.42
  275.3 3.0 fusion.41
  282.6 4.0 copy.188
  286.6 2.3 dynamic-slice_bitcast_fusion.5
  289.4 2.9 fusion.28.part_ref
  292.4 16.5 %scatter_tp.3 = f32[128,1536]{1,0:T(8,128)S(1)} custom-call(bf16[512,1536]{1,0:T(8,128)(2,1)S(1)} %fusion.28.part_ref), custom_call_target="tpu_custom_call" | custom-call | bytes 40000000 | tf_op jit(solution)/shard_map/scatter_tp/pallas_call | solution.py:176
  317.6 53.3 %all-reduce.1 = (f32[1536]{0:T(1024)}, f32[1536]{0:T(1024)}) all-reduce(f32[1536]{0:T(1024)S(1)} %get-tuple-element.12, f32[1536]{0:T(1024)S(1)} %copy-done.115), channel_id=1, replica_groups=mesh['dp'=4,'ep'=2,'tp'=4] {'dp','ep','tp'}, use_global_device_ids=true, to_apply=%region_18.19 | all-reduce | flops 3072 | bytes 24576 | tf_op jit(solution)/shard_map/psum | solution.py:452
  375.6 26.9 %collective-permute-done.5 = bf16[1,192,384]{2,1,0:T(8,128)(2,1)S(1)} collective-permute-done((bf16[1,192,384]{2,1,0:T(8,128)(2,1)S(1)}, bf16[1,192,384]{2,1,0:T(8,128)(2,1)S(1)}, u32[]{:S(2)}, u32[]{:S(2)}) %collective-permute-start.5) | collective-permute-done | bytes 147488 | tf_op jit(solution)/shard_map/ppermute | solution.py:209
  403.3 2.0 collective-permute-start.1
  410.8 2.6 collective-permute-start.15
  417.5 50.9 %collective-permute-done.1 = bf16[2,192,640]{2,1,0:T(8,128)(2,1)S(1)} collective-permute-done((bf16[2,192,640]{2,1,0:T(8,128)(2,1)S(1)}, bf16[2,192,640]{2,1,0:T(8,128)(2,1)S(1)}, u32[]{:S(2)}, u32[]{:S(2)}) %collective-permute-start.1) | collective-permute-done | bytes 491552 | tf_op jit(solution)/shard_map/ppermute | solution.py:209
  468.4 3.3 collective-permute-start.9
  473.6 45.1 %collective-permute-done.2 = bf16[1,192,640]{2,1,0:T(8,128)(2,1)S(1)} collective-permute-done((bf16[1,192,640]{2,1,0:T(8,128)(2,1)S(1)}, bf16[1,192,640]{2,1,0:T(8,128)(2,1)S(1)}, u32[]{:S(2)}, u32[]{:S(2)}) %collective-permute-start.2) | collective-permute-done | bytes 245792 | tf_op jit(solution)/shard_map/ppermute | solution.py:209
  518.6 3.4 collective-permute-start.11
  527.8 17.1 %collective-permute-done.11 = bf16[1,768,384]{1,2,0:T(8,128)(2,1)} collective-permute-done((bf16[1,768,384]{1,2,0:T(8,128)(2,1)}, bf16[1,768,384]{1,2,0:T(8,128)(2,1)}, u32[]{:S(2)}, u32[]{:S(2)}) %collective-permute-start.11) | collective-permute-done | bytes 589856 | tf_op jit(solution)/shard_map/ppermute | solution.py:209
  548.7 2.4 slice.187
  551.1 5.5 copy.214
  (429 shorter events, 122.9 us)
Async XLA Ops:
  7.2 36.1 %copy-start = (bf16[384,1536]{1,0:T(8,128)(2,1)S(1)}, bf16[384,1536]{1,0:T(8,128)(2,1)}, u32[]{:S(2)}) copy-start(bf16[384,1536]{1,0:T(8,128)(2,1)} %param.18) | copy-start | bytes 3538948
  7.2 104.2 %all-gather.2.cloned.1.call-start = ((), (), s32[]{:S(2)}) async-start(), calls=%async_computation | async-start | bytes 3833856 | tf_op jit(solution)/shard_map/all_gather | solution.py:284
  10.1 548.3 %all-reduce.4.cloned.1.call-start = ((), (), s32[]{:S(2)}) async-start(), calls=%async_computation.1 | async-start | bytes 294912 | tf_op jit(solution)/shard_map/psum | solution.py:452
  11.5 23.6 %copy-start.113 = (f32[1536]{0:T(1024)S(1)}, f32[1536]{0:T(1024)}, u32[]{:S(2)}) copy-start(f32[1536]{0:T(1024)} %param.15) | copy-start | bytes 18436
  13.8 22.0 %copy-start.62 = (bf16[1536,2,128]{0,2,1:T(8,128)(2,1)}, bf16[1536,2,128]{0,2,1:T(8,128)(2,1)S(1)}, u32[]{:S(2)}) copy-start(bf16[1536,2,128]{0,2,1:T(8,128)(2,1)S(1)} %copy.161) | copy-start | bytes 2359300
  43.3 17.5 %copy-start.92 = (bf16[2,64,3,512]{3,1,2,0:T(8,128)(2,1)}, bf16[2,64,3,512]{3,1,2,0:T(8,128)(2,1)S(1)}, u32[]{:S(2)}) copy-start(bf16[2,64,3,512]{3,1,2,0:T(8,128)(2,1)S(1)} %convolution_convert_fusion.15) | copy-start | bytes 1179652
  44.3 17.2 %copy-start.100 = (f32[1536]{0:T(1024)S(1)}, f32[1536]{0:T(1024)}, u32[]{:S(2)}) copy-start(f32[1536]{0:T(1024)} %param.19) | copy-start | bytes 18436
  61.5 23.7 %copy-start.116 = (f32[128]{0:T(128)}, f32[128]{0:T(128)S(1)}, u32[]{:S(2)}) copy-start(f32[128]{0:T(128)S(1)} %get-tuple-element.85) | copy-start | bytes 1540
  115.5 19.3 %copy-start.103 = (f32[1024,2]{0,1:T(2,128)}, f32[1024,2]{0,1:T(2,128)S(1)}, u32[]{:S(2)}) copy-start(f32[1024,2]{0,1:T(2,128)S(1)} %get-tuple-element.65) | copy-start | bytes 24580
  115.5 21.1 %copy-start.105 = (f32[1024,2]{0,1:T(2,128)}, f32[1024,2]{0,1:T(2,128)S(1)}, u32[]{:S(2)}) copy-start(f32[1024,2]{0,1:T(2,128)S(1)} %get-tuple-element.66) | copy-start | bytes 24580
  115.5 23.9 %copy-start.107 = (f32[1024,2]{0,1:T(2,128)}, f32[1024,2]{0,1:T(2,128)S(1)}, u32[]{:S(2)}) copy-start(f32[1024,2]{0,1:T(2,128)S(1)} %get-tuple-element.67) | copy-start | bytes 24580
  115.5 26.8 %copy-start.109 = (f32[1024,2]{0,1:T(2,128)}, f32[1024,2]{0,1:T(2,128)S(1)}, u32[]{:S(2)}) copy-start(f32[1024,2]{0,1:T(2,128)S(1)} %get-tuple-element.68) | copy-start | bytes 24580
  115.5 29.7 %copy-start.111 = (f32[1024,2]{0,1:T(2,128)}, f32[1024,2]{0,1:T(2,128)S(1)}, u32[]{:S(2)}) copy-start(f32[1024,2]{0,1:T(2,128)S(1)} %get-tuple-element.69) | copy-start | bytes 24580
  165.2 17.8 %copy-start.101 = (f32[1536]{0:T(1024)S(1)}, f32[1536]{0:T(1024)}, u32[]{:S(2)}) copy-start(f32[1536]{0:T(1024)} %param.19) | copy-start | bytes 18436
  165.3 17.8 %copy-start.117 = (f32[128]{0:T(128)S(1)}, f32[128]{0:T(128)}, u32[]{:S(2)}) copy-start(f32[128]{0:T(128)} %copy-done.116) | copy-start | bytes 1540
  165.3 18.6 %copy-start.61 = (bf16[128,1536]{1,0:T(8,128)(2,1)S(1)}, bf16[128,1536]{1,0:T(8,128)(2,1)}, u32[]{:S(2)}) copy-start(bf16[128,1536]{1,0:T(8,128)(2,1)} %param.23) | copy-start | bytes 1179652
  183.9 19.0 %slice-start = ((s8[6291456]{0:T(1024)(128)(4,1)}), s8[4194304]{0:T(1024)(128)(4,1)S(1)}, s32[]{:S(2)}) async-start(s8[6291456]{0:T(1024)(128)(4,1)} %bitcast.602), calls=%async_computation.2 | async-start | bytes 8388608
  238.0 22.0 %copy-start.64 = (bf16[1024,1536]{0,1:T(8,128)(2,1)S(1)}, bf16[1024,1536]{0,1:T(8,128)(2,1)}, u32[]{:S(2)}) copy-start(bf16[1024,1536]{0,1:T(8,128)(2,1)} %copy.264) | copy-start | bytes 9437188
  242.6 17.4 %copy-start.52 = (bf16[1024,2,2,128]{0,3,2,1:T(8,128)(2,1)S(1)}, bf16[1024,2,2,128]{0,3,2,1:T(8,128)(2,1)}, u32[]{:S(2)}) copy-start(bf16[1024,2,2,128]{0,3,2,1:T(8,128)(2,1)} %copy-done.51) | copy-start | bytes 3145732
  263.2 140.1 %collective-permute-start.6 = (bf16[2,768,384]{1,2,0:T(8,128)(2,1)}, bf16[2,768,384]{1,2,0:T(8,128)(2,1)}, u32[]{:S(2)}, u32[]{:S(2)}) collective-permute-start(bf16[2,768,384]{1,2,0:T(8,128)(2,1)} %dynamic-slice_bitcast_fusion.4), channel_id=1, source_target_pairs={{0,8},{8,0},{16,24},{24,16},{1,9},{9,1},{17,25},{25,17},{2,10},{10... | collective-permute-start | bytes 3538952 | tf_op jit(solution)/shard_map/ppermute | solution.py:209
  267.0 140.8 %collective-permute-start.14 = (bf16[2,768,384]{1,2,0:T(8,128)(2,1)}, bf16[2,768,384]{1,2,0:T(8,128)(2,1)}, u32[]{:S(2)}, u32[]{:S(2)}) collective-permute-start(bf16[2,768,384]{1,2,0:T(8,128)(2,1)} %dynamic-slice_bitcast_fusion), channel_id=1, source_target_pairs={{0,8},{8,0},{16,24},{24,16},{1,9},{9,1},{17,25},{25,17},{2,10},{10... | collective-permute-start | bytes 3538952 | tf_op jit(solution)/shard_map/ppermute | solution.py:209
  271.5 139.3 %collective-permute-start.12 = (bf16[2,768,384]{1,2,0:T(8,128)(2,1)}, bf16[2,768,384]{1,2,0:T(8,128)(2,1)}, u32[]{:S(2)}, u32[]{:S(2)}) collective-permute-start(bf16[2,768,384]{1,2,0:T(8,128)(2,1)} %dynamic-slice_bitcast_fusion.1), channel_id=1, source_target_pairs={{0,8},{8,0},{16,24},{24,16},{1,9},{9,1},{17,25},{25,17},{2,10},{10... | collective-permute-start | bytes 3538952 | tf_op jit(solution)/shard_map/ppermute | solution.py:209
  279.2 33.0 %collective-permute-start.3 = (bf16[4,192,384]{2,1,0:T(8,128)(2,1)}, bf16[4,192,384]{2,1,0:T(8,128)(2,1)}, u32[]{:S(2)}, u32[]{:S(2)}) collective-permute-start(bf16[4,192,384]{2,1,0:T(8,128)(2,1)} %dynamic-slice_bitcast_fusion.6), channel_id=1, source_target_pairs={{0,4},{4,0},{1,5},{5,1},{2,6},{6,2},{3,7},{7,3},{8,12},{12,8},{9,1... | collective-permute-start | bytes 1769480 | tf_op jit(solution)/shard_map/ppermute | solution.py:441
  288.9 20.0 %copy-start.119 = (f32[128]{0:T(128)S(1)}, f32[128]{0:T(128)}, u32[]{:S(2)}) copy-start(f32[128]{0:T(128)} %get-tuple-element.84) | copy-start | bytes 1540
  288.9 83.8 %collective-permute-start = (bf16[4,192,640]{2,1,0:T(8,128)(2,1)}, bf16[4,192,640]{2,1,0:T(8,128)(2,1)}, u32[]{:S(2)}, u32[]{:S(2)}) collective-permute-start(bf16[4,192,640]{2,1,0:T(8,128)(2,1)} %dynamic-slice_bitcast_fusion.5), channel_id=1, source_target_pairs={{0,4},{4,0},{1,5},{5,1},{2,6},{6,2},{3,7},{7,3},{8,12},{12,8},{9,1... | collective-permute-start | bytes 2949128 | tf_op jit(solution)/shard_map/ppermute | solution.py:441
  292.4 16.9 %copy-start.69 = (bf16[4,512,384]{1,2,0:T(8,128)(2,1)S(1)}, bf16[4,512,384]{1,2,0:T(8,128)(2,1)}, u32[]{:S(2)}) copy-start(bf16[4,512,384]{1,2,0:T(8,128)(2,1)} %fusion.41) | copy-start | bytes 4718596
  292.4 16.9 %copy-start.81 = (bf16[4,256,384]{1,2,0:T(8,128)(2,1)S(1)}, bf16[4,256,384]{1,2,0:T(8,128)(2,1)}, u32[]{:S(2)}) copy-start(bf16[4,256,384]{1,2,0:T(8,128)(2,1)} %fusion.46) | copy-start | bytes 2359300
  313.6 57.3 %copy-start.16 = (bf16[4,768,384]{1,2,0:T(8,128)(2,1)S(1)}, bf16[4,768,384]{1,2,0:T(8,128)(2,1)}, u32[]{:S(2)}) copy-start(bf16[4,768,384]{1,2,0:T(8,128)(2,1)} %pad_maximum_fusion.1) | copy-start | bytes 7077892
  313.6 57.4 %collective-permute-start.4 = (bf16[2,192,384]{2,1,0:T(8,128)(2,1)S(1)}, bf16[2,192,384]{2,1,0:T(8,128)(2,1)S(1)}, u32[]{:S(2)}, u32[]{:S(2)}) collective-permute-start(bf16[2,192,384]{2,1,0:T(8,128)(2,1)S(1)} %dynamic-slice_bitcast_fusion.8), channel_id=1, source_target_pairs={{0,8},{8,0},{16,24},{24,16},{1,9},{9,1},{17,25},{25,17},{2,10},{10... | collective-permute-start | bytes 884744 | tf_op jit(solution)/shard_map/ppermute | solution.py:209
  371.0 31.5 %copy-start.70 = (bf16[2,768,384]{1,2,0:T(8,128)(2,1)S(1)}, bf16[2,768,384]{1,2,0:T(8,128)(2,1)}, u32[]{:S(2)}) copy-start(bf16[2,768,384]{1,2,0:T(8,128)(2,1)} %dynamic-slice_bitcast_fusion.2) | copy-start | bytes 3538948
  371.0 45.0 %collective-permute-start.8 = (bf16[2,768,384]{1,2,0:T(8,128)(2,1)S(1)}, bf16[2,768,384]{1,2,0:T(8,128)(2,1)S(1)}, u32[]{:S(2)}, u32[]{:S(2)}) collective-permute-start(bf16[2,768,384]{1,2,0:T(8,128)(2,1)S(1)} %dynamic-slice_bitcast_fusion.3), channel_id=1, source_target_pairs={{0,8},{8,0},{16,24},{24,16},{1,9},{9,1},{17,25},{25,17},{2,10},{10... | collective-permute-start | bytes 3538952 | tf_op jit(solution)/shard_map/ppermute | solution.py:209
  372.7 32.6 %copy-start.15 = (bf16[4,768,384]{1,2,0:T(8,128)(2,1)S(1)}, bf16[4,768,384]{1,2,0:T(8,128)(2,1)}, u32[]{:S(2)}) copy-start(bf16[4,768,384]{1,2,0:T(8,128)(2,1)} %copy-done.14) | copy-start | bytes 7077892
  372.7 29.8 %collective-permute-start.5 = (bf16[1,192,384]{2,1,0:T(8,128)(2,1)S(1)}, bf16[1,192,384]{2,1,0:T(8,128)(2,1)S(1)}, u32[]{:S(2)}, u32[]{:S(2)}) collective-permute-start(bf16[1,192,384]{2,1,0:T(8,128)(2,1)S(1)} %constant_dynamic-slice_fusion.10), channel_id=1, source_target_pairs={{0,16},{8,24},{16,0},{24,8},{1,17},{9,25},{17,1},{25,9},{2,18},{10... | collective-permute-start | bytes 442376 | tf_op jit(solution)/shard_map/ppermute | solution.py:209
  375.6 32.6 %copy-start.13 = (bf16[4,768,384]{1,2,0:T(8,128)(2,1)S(1)}, bf16[4,768,384]{1,2,0:T(8,128)(2,1)}, u32[]{:S(2)}) copy-start(bf16[4,768,384]{1,2,0:T(8,128)(2,1)} %copy-done.12) | copy-start | bytes 7077892
  402.5 69.4 %collective-permute-start.10 = (bf16[2,768,384]{1,2,0:T(8,128)(2,1)S(1)}, bf16[2,768,384]{1,2,0:T(8,128)(2,1)S(1)}, u32[]{:S(2)}, u32[]{:S(2)}) collective-permute-start(bf16[2,768,384]{1,2,0:T(8,128)(2,1)S(1)} %copy-done.70), channel_id=1, source_target_pairs={{0,8},{8,0},{16,24},{24,16},{1,9},{9,1},{17,25},{25,17},{2,10},{10... | collective-permute-start | bytes 3538952 | tf_op jit(solution)/shard_map/ppermute | solution.py:209
  403.3 65.2 %collective-permute-start.1 = (bf16[2,192,640]{2,1,0:T(8,128)(2,1)S(1)}, bf16[2,192,640]{2,1,0:T(8,128)(2,1)S(1)}, u32[]{:S(2)}, u32[]{:S(2)}) collective-permute-start(bf16[2,192,640]{2,1,0:T(8,128)(2,1)S(1)} %dynamic-slice_bitcast_fusion.7), channel_id=1, source_target_pairs={{0,8},{8,0},{16,24},{24,16},{1,9},{9,1},{17,25},{25,17},{2,10},{10... | collective-permute-start | bytes 1474568 | tf_op jit(solution)/shard_map/ppermute | solution.py:209
  408.1 117.1 %collective-permute-start.7 = (bf16[1,768,384]{1,2,0:T(8,128)(2,1)}, bf16[1,768,384]{1,2,0:T(8,128)(2,1)}, u32[]{:S(2)}, u32[]{:S(2)}) collective-permute-start(bf16[1,768,384]{1,2,0:T(8,128)(2,1)} %constant_dynamic-slice_fusion.9), channel_id=1, source_target_pairs={{0,16},{8,24},{16,0},{24,8},{1,17},{9,25},{17,1},{25,9},{2,18},{10... | collective-permute-start | bytes 1769480 | tf_op jit(solution)/shard_map/ppermute | solution.py:209
  410.8 136.5 %collective-permute-start.15 = (bf16[1,768,384]{1,2,0:T(8,128)(2,1)}, bf16[1,768,384]{1,2,0:T(8,128)(2,1)}, u32[]{:S(2)}, u32[]{:S(2)}) collective-permute-start(bf16[1,768,384]{1,2,0:T(8,128)(2,1)} %constant_dynamic-slice_fusion.5), channel_id=1, source_target_pairs={{0,16},{8,24},{16,0},{24,8},{1,17},{9,25},{17,1},{25,9},{2,18},{10... | collective-permute-start | bytes 1769480 | tf_op jit(solution)/shard_map/ppermute | solution.py:209
  416.0 56.0 %copy-start.18 = (bf16[4,768,384]{1,2,0:T(8,128)(2,1)S(1)}, bf16[4,768,384]{1,2,0:T(8,128)(2,1)}, u32[]{:S(2)}) copy-start(bf16[4,768,384]{1,2,0:T(8,128)(2,1)} %copy-done.17) | copy-start | bytes 7077892
  416.0 130.1 %collective-permute-start.13 = (bf16[1,768,384]{1,2,0:T(8,128)(2,1)}, bf16[1,768,384]{1,2,0:T(8,128)(2,1)}, u32[]{:S(2)}, u32[]{:S(2)}) collective-permute-start(bf16[1,768,384]{1,2,0:T(8,128)(2,1)} %constant_dynamic-slice_fusion.6), channel_id=1, source_target_pairs={{0,16},{8,24},{16,0},{24,8},{1,17},{9,25},{17,1},{25,9},{2,18},{10... | collective-permute-start | bytes 1769480 | tf_op jit(solution)/shard_map/ppermute | solution.py:209
  416.6 55.7 %copy-start.39 = (bf16[2,768,384]{1,2,0:T(8,128)(2,1)}, bf16[2,768,384]{1,2,0:T(8,128)(2,1)S(1)}, u32[]{:S(2)}) copy-start(bf16[2,768,384]{1,2,0:T(8,128)(2,1)S(1)} %fusion.32) | copy-start | bytes 3538948
  468.4 58.1 %collective-permute-start.9 = (bf16[1,768,384]{1,2,0:T(8,128)(2,1)}, bf16[1,768,384]{1,2,0:T(8,128)(2,1)}, u32[]{:S(2)}, u32[]{:S(2)}) collective-permute-start(bf16[1,768,384]{1,2,0:T(8,128)(2,1)} %constant_dynamic-slice_fusion.8), channel_id=1, source_target_pairs={{0,16},{8,24},{16,0},{24,8},{1,17},{9,25},{17,1},{25,9},{2,18},{10... | collective-permute-start | bytes 1769480 | tf_op jit(solution)/shard_map/ppermute | solution.py:209
  471.9 46.7 %collective-permute-start.2 = (bf16[1,192,640]{2,1,0:T(8,128)(2,1)S(1)}, bf16[1,192,640]{2,1,0:T(8,128)(2,1)S(1)}, u32[]{:S(2)}, u32[]{:S(2)}) collective-permute-start(bf16[1,192,640]{2,1,0:T(8,128)(2,1)S(1)} %constant_dynamic-slice_fusion.11), channel_id=1, source_target_pairs={{0,16},{8,24},{16,0},{24,8},{1,17},{9,25},{17,1},{25,9},{2,18},{10... | collective-permute-start | bytes 737288 | tf_op jit(solution)/shard_map/ppermute | solution.py:209
  472.4 52.9 %copy-start.36 = (bf16[2,768,384]{1,2,0:T(8,128)(2,1)S(1)}, bf16[2,768,384]{1,2,0:T(8,128)(2,1)}, u32[]{:S(2)}) copy-start(bf16[2,768,384]{1,2,0:T(8,128)(2,1)} %copy-done.35) | copy-start | bytes 3538948
  473.6 52.9 %copy-start.40 = (bf16[2,768,384]{1,2,0:T(8,128)(2,1)S(1)}, bf16[2,768,384]{1,2,0:T(8,128)(2,1)}, u32[]{:S(2)}) copy-start(bf16[2,768,384]{1,2,0:T(8,128)(2,1)} %copy-done.39) | copy-start | bytes 3538948
  518.6 26.3 %collective-permute-start.11 = (bf16[1,768,384]{1,2,0:T(8,128)(2,1)}, bf16[1,768,384]{1,2,0:T(8,128)(2,1)}, u32[]{:S(2)}, u32[]{:S(2)}) collective-permute-start(bf16[1,768,384]{1,2,0:T(8,128)(2,1)} %constant_dynamic-slice_fusion.7), channel_id=1, source_target_pairs={{0,16},{8,24},{16,0},{24,8},{1,17},{9,25},{17,1},{25,9},{2,18},{10... | collective-permute-start | bytes 1769480 | tf_op jit(solution)/shard_map/ppermute | solution.py:209
  525.2 19.7 %copy-start.42 = (bf16[2,768,384]{1,2,0:T(8,128)(2,1)S(1)}, bf16[2,768,384]{1,2,0:T(8,128)(2,1)}, u32[]{:S(2)}) copy-start(bf16[2,768,384]{1,2,0:T(8,128)(2,1)} %copy-done.41) | copy-start | bytes 3538948
  526.5 19.6 %copy-start.38 = (bf16[2,768,384]{1,2,0:T(8,128)(2,1)S(1)}, bf16[2,768,384]{1,2,0:T(8,128)(2,1)}, u32[]{:S(2)}) copy-start(bf16[2,768,384]{1,2,0:T(8,128)(2,1)} %copy-done.37) | copy-start | bytes 3538948
  (105 other events, 305.2 us)
Sparse Core Ops, SparseCore 0:
  10.2 40.4 all-gather.1
  232.1 124.9 all-reduce.3
